TPU v7x, 512 devices: a whole 4x4x16 slice. The times are simulated.
512 devices in a mesh: pop: 64 (over y_lo, z, core), shard: 8 (over x, y_hi).
Axes of the slice: x: 4, y: 4 (y_hi: 2, y_lo: 2; y = y_hi * 2 + y_lo), z: 16, core: 2. Of those that a mesh axis runs over, the one named last changes fastest.
Arguments:
- hidden: bfloat16 [8192, 4096], P('pop'), may hold values from -6 to 6
- weight: bfloat16 [4096, 14336], P('pop', 'shard'), may hold values from -0.09375 to 0.09375
- left_factors: bfloat16 [512, 4096], P('pop'), may hold values from -6 to 6
- right_factors: bfloat16 [512, 14336], P('pop', 'shard'), may hold values from -6 to 6
- target: bfloat16 [8192, 14336], P('pop', 'shard'), may hold values from -6 to 6
Outputs:
- up_out: bfloat16 [8192, 14336], P('pop', 'shard')
- step: float32 [4096, 14336], P('pop', 'shard')
- fitness: float32 [512], P('pop')
All inputs are finite; a program needn't handle non-finite values.
Results may differ from a plain program's by a relative error of at most 0.001.
Values may be sent and summed in bfloat16 or wider, within the bound.
No kernel may reach another device: no remote copies, remote signals or barrier semaphores. Data moves between devices by JAX's collectives and lax.ppermute only.
A program may use at most 64 MiB of HBM per device.

v0:
```python
import math
import jax
import jax.numpy as jnp
from jax import lax
from jax.sharding import PartitionSpec as P

noise_scale = 0.5
spread_eps = 1e-05


def split_parts(values):
    high = values.astype(jnp.bfloat16)
    kept = lax.optimization_barrier(high)
    low = (values - kept.astype(jnp.float32)).astype(jnp.bfloat16)
    return (high, low)


def local(hidden, weight, left_factors, right_factors, target):
    local_members = left_factors.shape[0]
    row_count = hidden.shape[0]
    token_count = row_count // local_members
    feature_count = hidden.shape[1]
    local_cols = weight.shape[1]
    member_count = local_members * lax.axis_size("pop")
    base_out = jnp.dot(
        hidden,
        lax.all_gather(weight, "pop", axis=0, tiled=True),
        preferred_element_type=jnp.float32,
    )
    grouped = hidden.reshape(local_members, token_count, feature_count)
    projected = jnp.einsum(
        "mtd,md->mt", grouped, left_factors, preferred_element_type=jnp.float32
    ) / math.sqrt(feature_count)
    right_wide = right_factors.astype(jnp.float32)
    perturbed = (
        base_out.reshape(local_members, token_count, local_cols)
        + noise_scale * projected[:, :, None] * right_wide[:, None, :]
    )
    up_out = perturbed.astype(jnp.bfloat16).reshape(row_count, local_cols)
    directions = target.reshape(local_members, token_count, local_cols).astype(jnp.float32)
    partial_value = jnp.sum(jax.nn.silu(perturbed) * directions, axis=(1, 2))
    reward = lax.psum(partial_value, "shard")
    mean_reward = lax.psum(jnp.sum(reward), "pop") / member_count
    centered = reward - mean_reward
    spread = lax.psum(jnp.sum(centered * centered), "pop") / member_count
    fitness = (reward - mean_reward) / jnp.sqrt(spread + spread_eps)
    weighted = left_factors.astype(jnp.float32) * fitness[:, None]
    weighted_all = lax.all_to_all(weighted, "pop", split_axis=1, concat_axis=0, tiled=True)
    weighted_high, weighted_low = split_parts(weighted_all)
    contract = (((0,), (0,)), ((), ()))
    portion = lax.all_gather(right_factors, "pop", axis=0, tiled=True)
    upper = lax.dot_general(weighted_high, portion, contract, preferred_element_type=jnp.float32)
    lower = lax.dot_general(weighted_low, portion, contract, preferred_element_type=jnp.float32)
    summed = upper + lower
    step = summed / math.sqrt(member_count)
    return (up_out, step, fitness)


def solution(mesh):
    in_specs = (
        P("pop", None),
        P("pop", "shard"),
        P("pop", None),
        P("pop", "shard"),
        P("pop", "shard"),
    )
    out_specs = (P("pop", "shard"), P("pop", "shard"), P("pop"))
    return jax.shard_map(local, mesh=mesh, in_specs=in_specs, out_specs=out_specs, check_vma=False)
```

profile of v0, /device:TPU:1, one launch (start us, length us, event | category | flops | bytes accessed | tf_op | source)
XLA Modules:
  0.0 432.2 jit_solution(2508791868741130458)
XLA Ops:
  7.2 0.0 copy-start
  7.2 0.0 copy-start.4
  7.2 0.0 all-gather.3.cloned.1.call-start
  7.2 0.7 all-gather.3.cloned.1.call-update
  7.9 0.0 all-gather.5.cloned.1.call-start
  8.0 0.7 all-gather.5.cloned.1.call-update
  8.7 0.8 convert_element_type.23
  9.4 0.0 copy-done
  9.4 1.3 fusion.3
  10.8 0.1 mul.48
  10.8 0.1 bitcast_multiply_fusion
  11.0 0.0 copy-start.2
  11.0 142.6 %all-gather.3.cloned.1.call-done = bf16[4096,1792]{1,0:T(8,128)(2,1)} async-done(((bf16[64,1792]{1,0:T(8,128)(2,1)}), bf16[4096,1792]{1,0:T(8,128)(2,1)}) %all-gather.3.cloned.1.call-update) | async-done | bytes 14680080 | tf_op jit(solution)/shard_map/all_gather | solution.py:27
  153.6 0.0 copy-done.4
  153.6 8.3 %multiply_reduce_fusion = (f32[128]{0:T(128)S(1)}, bf16[128,1792]{1,0:T(8,128)(2,1)}) fusion(bf16[128,1792]{1,0:T(8,128)(2,1)S(1)} %copy-done.4, f32[128,1792]{1,0:T(8,128)S(1)} %bitcast_multiply_fusion, bf16[128,4096]{1,0:T(8,128)(2,1)S(1)} %copy-done, bf16[4096,1792]{1,0:T(8,128)(2,1)} %all-gather.3.cloned.1.call-done), kind=kOutput, calls=%fused_computation.4 | convolution fusion | flops 1881112448 | bytes 17564160 | tf_op jit(solution)/shard_map/dot_general | solution.py:25
  161.9 0.1 reduce_sum.35
  161.9 0.1 reduce_sum.36
  162.1 20.1 %psum.21 = f32[8]{0:T(128)S(1)} all-reduce(f32[8]{0:T(128)S(1)} %reduce_sum.36), channel_id=1, replica_groups=mesh['pop'=64,'shard'=8] {'shard'}, use_global_device_ids=true, to_apply=%region_2.3 | all-reduce | flops 8 | bytes 64 | tf_op jit(solution)/shard_map/psum | solution.py:42
  182.2 0.6 reduce_sum.37
  182.8 108.7 %psum.22 = f32[]{:T(128)} all-reduce(f32[]{:T(128)} %reduce_sum.37), channel_id=1, replica_groups=mesh['pop'=64,'shard'=8] {'pop'}, use_global_device_ids=true, to_apply=%region_4.5 | all-reduce | flops 1 | bytes 8 | tf_op jit(solution)/shard_map/psum | solution.py:43
  292.1 0.6 multiply_reduce_fusion.1
  292.7 105.3 %psum.23 = f32[]{:T(128)} all-reduce(f32[]{:T(128)} %multiply_reduce_fusion.1), channel_id=1, replica_groups=mesh['pop'=64,'shard'=8] {'pop'}, use_global_device_ids=true, to_apply=%region_6.7 | all-reduce | flops 1 | bytes 8 | tf_op jit(solution)/shard_map/psum | solution.py:45
  398.7 0.0 copy-done.2
  398.7 0.0 copy-start.3
  398.8 0.1 convert_multiply_fusion
  398.8 0.1 all_to_all.14
  398.9 0.2 copy.14
  399.1 0.2 reshape.28
  399.3 21.1 %all_to_all.19 = f32[64,1,512]{2,1,0:T(1,128)S(1)} all-to-all(f32[64,1,512]{2,1,0:T(1,128)S(1)} %reshape.28), channel_id=1, replica_groups=mesh['pop'=64,'shard'=8] {'pop'}, dimensions={0} | all-to-all | bytes 262144 | tf_op jit(solution)/shard_map/all_to_all | solution.py:48
  420.4 0.5 broadcast.14
  420.9 1.0 reduce.2
  421.9 0.1 reshape.29
  422.0 0.0 all-gather.5.cloned.1.call-done
  422.0 0.0 copy-start.1
  422.0 2.1 fusion.6
  424.1 0.0 copy-done.3
  424.1 0.0 copy-done.1
  424.2 1.2 fusion
  (3 shorter events, 0.0 us)
Async XLA Ops:
  7.2 2.3 copy-start
  7.2 146.4 %copy-start.4 = (bf16[128,1792]{1,0:T(8,128)(2,1)S(1)}, bf16[128,1792]{1,0:T(8,128)(2,1)}, u32[]{:S(2)}) copy-start(bf16[128,1792]{1,0:T(8,128)(2,1)} %param.9) | copy-start | bytes 1376260
  7.2 146.4 %all-gather.3.cloned.1.call-start = ((), (), s32[]{:S(2)}) async-start(), calls=%async_computation.1 | async-start | bytes 14909440 | tf_op jit(solution)/shard_map/all_gather | solution.py:27
  7.9 414.1 %all-gather.5.cloned.1.call-start = ((), (), s32[]{:S(2)}) async-start(), calls=%async_computation.2 | async-start | bytes 1863680 | tf_op jit(solution)/shard_map/all_gather | solution.py:51
  11.0 387.7 %copy-start.2 = (bf16[8,4096]{1,0:T(8,128)(2,1)S(1)}, bf16[8,4096]{1,0:T(8,128)(2,1)}, u32[]{:S(2)}) copy-start(bf16[8,4096]{1,0:T(8,128)(2,1)} %param.7) | copy-start | bytes 196612
  398.7 25.4 %copy-start.3 = (f32[8]{0:T(128)}, f32[8]{0:T(128)S(1)}, u32[]{:S(2)}) copy-start(f32[8]{0:T(128)S(1)} %subtract_divide_fusion) | copy-start | bytes 100
  422.0 2.1 copy-start.1
Sparse Core Ops, SparseCore 0:
  10.2 143.3 all-gather.2
  155.7 118.4 all-gather.4
where the time goes:
time: 433 us; the launch traced here: 432 us
  blocking collectives  255 us (59%)
  waiting for transfers between devices  144 us (33%)
  between operations  15.5 us (4%)
  matrix products  12.9 us (3%)
    all_gather x1, waiting for transfers between devices, local(): lax.all_gather(weight, 'pop', axis=0, tiled=True)  143 us
    psum x1, blocking collectives, local(): mean_reward = lax.psum(jnp.sum(reward), 'pop') / member_count  109 us
    psum x1, blocking collectives, local(): spread = lax.psum(jnp.sum(centered * centered), 'pop') / member_count  105 us
    all_to_all x1, blocking collectives, local(): lax.all_to_all(weighted, 'pop', split_axis=1, concat_axis=0, tiled=True)  21.1 us
    psum x1, blocking collectives, local(): reward = lax.psum(partial_value, 'shard')  20.1 us
  transfers between devices with their start and end apart: 2, of which 1 were waited for; matrix products, arithmetic and copies ran while one was open for 3% of the time, Pallas kernels for 0%

commit v1 on v0

--- a/solution.py
+++ b/solution.py
@@ -24,7 +24,9 @@
     member_count = local_members * lax.axis_size("pop")
     base_out = jnp.dot(
         hidden,
-        lax.all_gather(weight, "pop", axis=0, tiled=True),
+        jnp.concatenate(
+            lax.all_to_all(jnp.stack([weight] * lax.axis_size("pop")), "pop", 0, 0), axis=0
+        ),
         preferred_element_type=jnp.float32,
     )
     grouped = hidden.reshape(local_members, token_count, feature_count)

time: 433 us -> 959 us (2.21)
  waiting for transfers between devices: 144 us -> 645 us
  starting transfers between devices: 0.08 us -> 18.5 us
    all_to_all x0 -> x1, waiting for transfers between devices: none -> 644 us  [local(): lax.all_to_all(jnp.stack([weight] * lax.axis_size('pop')), 'pop', 0, 0)]
    all_gather x1 -> x0, waiting for transfers between devices: 143 us -> none  [local(): lax.all_gather(weight, 'pop', axis=0, tiled=True)]
    all_to_all x0 -> x1, starting transfers between devices: none -> 18.5 us  [local(): lax.all_to_all(jnp.stack([weight] * lax.axis_size('pop')), 'pop', 0, 0)]
  transfers between devices with their start and end apart: 2 -> 2, of which waited for: 1 -> 1; matrix products, arithmetic and copies ran while one was open for 3% -> 1% of each run, Pallas kernels for 0% -> 0%
where the time goes in v1:
time: 959 us; the launch traced here: 958 us
  waiting for transfers between devices  645 us (67%)
  blocking collectives  256 us (27%)
  starting transfers between devices  18.5 us (2%)
  between operations  15.5 us (2%)
  matrix products  12.1 us (1%)
    all_to_all x1, waiting for transfers between devices, local(): lax.all_to_all(jnp.stack([weight] * lax.axis_size('pop')), 'pop', 0, 0)  644 us
    psum x1, blocking collectives, local(): mean_reward = lax.psum(jnp.sum(reward), 'pop') / member_count  109 us
    psum x1, blocking collectives, local(): spread = lax.psum(jnp.sum(centered * centered), 'pop') / member_count  105 us
    all_to_all x1, blocking collectives, local(): lax.all_to_all(weighted, 'pop', split_axis=1, concat_axis=0, tiled=True)  21.1 us
    psum x1, blocking collectives, local(): reward = lax.psum(partial_value, 'shard')  20.3 us
  transfers between devices with their start and end apart: 2, of which 1 were waited for; matrix products, arithmetic and copies ran while one was open for 1% of the time, Pallas kernels for 0%

profile of v1, /device:TPU:1, one launch (start us, length us, event | category | flops | bytes accessed | tf_op | source)
XLA Modules:
  0.0 958.4 jit_solution(2872921427562330232)
XLA Ops:
  7.2 0.0 copy-start
  7.2 8.0 stack.2
  15.2 0.0 copy-start.3
  15.2 0.0 copy-start.2
  15.2 0.0 copy-start.5
  15.2 18.5 %all-to-all-start = ((bf16[64,64,1792]{2,1,0:T(8,128)(2,1)}), bf16[64,64,1792]{2,1,0:T(8,128)(2,1)}, u32[]{:S(2)}, u32[]{:S(2)}) async-start(bf16[64,64,1792]{2,1,0:T(8,128)(2,1)} %stack.2), calls=%async_computation | async-start | bytes 29360128 | tf_op jit(solution)/shard_map/all_to_all | solution.py:28
  33.7 0.0 all-gather.2.cloned.1.call-start
  33.7 0.7 all-gather.2.cloned.1.call-update
  34.4 0.0 copy-done
  34.4 0.0 copy-done.3
  34.4 0.5 fusion.4
  34.9 0.0 copy-done.2
  34.9 644.2 %all-to-all-done = bf16[64,64,1792]{2,1,0:T(8,128)(2,1)} async-done(((bf16[64,64,1792]{2,1,0:T(8,128)(2,1)}), bf16[64,64,1792]{2,1,0:T(8,128)(2,1)}, u32[]{:S(2)}, u32[]{:S(2)}) %all-to-all-start) | async-done | bytes 14680096 | tf_op jit(solution)/shard_map/all_to_all | solution.py:28
  679.1 0.0 copy-done.5
  679.1 8.3 fusion.1
  687.4 20.3 %psum.21 = f32[8]{0:T(128)S(1)} all-reduce(f32[8]{0:T(128)S(1)} %get-tuple-element.3), channel_id=1, replica_groups=mesh['pop'=64,'shard'=8] {'shard'}, use_global_device_ids=true, to_apply=%region_1.2 | all-reduce | flops 8 | bytes 64 | tf_op jit(solution)/shard_map/psum | solution.py:44
  707.6 0.6 reduce_sum.28
  708.2 109.4 %psum.22 = f32[]{:T(128)} all-reduce(f32[]{:T(128)} %reduce_sum.28), channel_id=1, replica_groups=mesh['pop'=64,'shard'=8] {'pop'}, use_global_device_ids=true, to_apply=%region_3.4 | all-reduce | flops 1 | bytes 8 | tf_op jit(solution)/shard_map/psum | solution.py:45
  818.3 0.6 multiply_reduce_fusion
  818.9 105.3 %psum.23 = f32[]{:T(128)} all-reduce(f32[]{:T(128)} %multiply_reduce_fusion), channel_id=1, replica_groups=mesh['pop'=64,'shard'=8] {'pop'}, use_global_device_ids=true, to_apply=%region_5.6 | all-reduce | flops 1 | bytes 8 | tf_op jit(solution)/shard_map/psum | solution.py:47
  924.9 0.0 copy-start.4
  924.9 0.1 convert_multiply_fusion.1
  925.0 0.1 all_to_all.18
  925.1 0.2 copy.14
  925.3 0.2 reshape.33
  925.5 21.1 %all_to_all.24 = f32[64,1,512]{2,1,0:T(1,128)S(1)} all-to-all(f32[64,1,512]{2,1,0:T(1,128)S(1)} %reshape.33), channel_id=1, replica_groups=mesh['pop'=64,'shard'=8] {'pop'}, dimensions={0} | all-to-all | bytes 262144 | tf_op jit(solution)/shard_map/all_to_all | solution.py:50
  946.6 0.5 broadcast.11
  947.1 0.9 reduce
  948.0 0.1 reshape.34
  948.2 0.0 all-gather.2.cloned.1.call-done
  948.2 0.0 copy-start.1
  948.2 2.1 fusion.7
  950.3 0.0 copy-done.4
  950.3 0.0 copy-done.1
  950.3 1.2 fusion
  (4 shorter events, 0.0 us)
Async XLA Ops:
  7.2 27.2 %copy-start = (bf16[128,4096]{1,0:T(8,128)(2,1)S(1)}, bf16[128,4096]{1,0:T(8,128)(2,1)}, u32[]{:S(2)}) copy-start(bf16[128,4096]{1,0:T(8,128)(2,1)} %param.5) | copy-start | bytes 3145732
  15.2 19.2 %copy-start.3 = (bf16[8,4096]{1,0:T(8,128)(2,1)S(1)}, bf16[8,4096]{1,0:T(8,128)(2,1)}, u32[]{:S(2)}) copy-start(bf16[8,4096]{1,0:T(8,128)(2,1)} %param.7) | copy-start | bytes 196612
  15.2 19.7 %copy-start.2 = (bf16[8,1792]{1,0:T(8,128)(2,1)S(1)}, bf16[8,1792]{1,0:T(8,128)(2,1)}, u32[]{:S(2)}) copy-start(bf16[8,1792]{1,0:T(8,128)(2,1)} %param.8) | copy-start | bytes 86020
  15.2 663.9 %copy-start.5 = (bf16[128,1792]{1,0:T(8,128)(2,1)S(1)}, bf16[128,1792]{1,0:T(8,128)(2,1)}, u32[]{:S(2)}) copy-start(bf16[128,1792]{1,0:T(8,128)(2,1)} %param.9) | copy-start | bytes 1376260
  15.2 663.9 %all-to-all-start = ((bf16[64,64,1792]{2,1,0:T(8,128)(2,1)}), bf16[64,64,1792]{2,1,0:T(8,128)(2,1)}, u32[]{:S(2)}, u32[]{:S(2)}) async-start(bf16[64,64,1792]{2,1,0:T(8,128)(2,1)} %stack.2), calls=%async_computation | async-start | bytes 29360128 | tf_op jit(solution)/shard_map/all_to_all | solution.py:28
  33.7 914.5 %all-gather.2.cloned.1.call-start = ((), (), s32[]{:S(2)}) async-start(), calls=%async_computation.2 | async-start | bytes 1863680 | tf_op jit(solution)/shard_map/all_gather | solution.py:53
  924.9 25.4 %copy-start.4 = (f32[8]{0:T(128)}, f32[8]{0:T(128)S(1)}, u32[]{:S(2)}) copy-start(f32[8]{0:T(128)S(1)} %subtract_divide_fusion) | copy-start | bytes 100
  948.2 2.1 copy-start.1
Sparse Core Ops, SparseCore 0:
  36.6 179.2 all-gather.1
